TPU v7x, 32 devices: a whole 2x2x4 slice. The times are simulated.
32 devices in a mesh: scan: 4 (over y, x), det: 8 (over z, core).
Axes of the slice: x: 2, y: 2, z: 4, core: 2. Of those that a mesh axis runs over, the one named last changes fastest.
Arguments:
- data: float32 [2, 512, 2, 256, 256], P(None, 'scan', None, 'det'), may hold values from -6 to 6
- wigner: float32 [2, 512, 2, 256, 256], P(None, ('scan', 'det')), may hold values from -6 to 6
Outputs:
- deconvolved: float32 [2, 512, 2, 256, 256], P(None, 'scan', None, 'det')
All inputs are finite; a program needn't handle non-finite values.
Results may differ from a plain program's by a relative error of at most 0.0001.
Values sent between devices are 32-bit elements; how exact they have to be, the bound alone decides.
A program may use at most 192 MiB of HBM per device.

v0:
```python
import math

import jax
import jax.numpy as jnp
from jax import lax
from jax.sharding import PartitionSpec as P

eps_wiener = 0.1


def tables(count, sign):
    indices = jnp.arange(count, dtype=jnp.int32)
    product = indices[:, None] * indices[None, :] % count
    phases = product.astype(jnp.float32) * (2.0 * math.pi / count)
    norm_scale = 1.0 / math.sqrt(count)
    return (jnp.cos(phases) * norm_scale, sign * jnp.sin(phases) * norm_scale)


def product_form(form, left, right):
    return jnp.einsum(form, left, right, precision=lax.Precision.HIGHEST)


def pair_right(real_in, imag_in, form, cosine, sines):
    real_out = product_form(form, real_in, cosine) - product_form(form, imag_in, sines)
    imag_out = product_form(form, real_in, sines) + product_form(form, imag_in, cosine)
    return (real_out, imag_out)


def pair_left(cosine, sines, real_in, imag_in):
    real_out = jnp.dot(cosine, real_in, precision=lax.Precision.HIGHEST) - jnp.dot(
        sines, imag_in, precision=lax.Precision.HIGHEST
    )
    imag_out = jnp.dot(cosine, imag_in, precision=lax.Precision.HIGHEST) + jnp.dot(
        sines, real_in, precision=lax.Precision.HIGHEST
    )
    return (real_out, imag_out)


def shards(data, wigner):
    detector = data.shape[4]
    freq_count = data.shape[2]
    local_rows = data.shape[3]
    rows_total = data.shape[1] * lax.axis_size("scan")
    inv_cos, inv_sin = tables(detector, 1.0)
    fwd_cos, fwd_sin = tables(detector, -1.0)
    row_cos, row_sin = tables(rows_total, -1.0)
    space_real, space_imag = pair_right(data[0], data[1], "rfab,by->rfay", inv_cos, inv_sin)
    flat_cols = freq_count * local_rows * detector
    space_real = space_real.reshape(data.shape[1], flat_cols)
    space_imag = space_imag.reshape(data.shape[1], flat_cols)
    whole_real, whole_imag = (
        lax.all_to_all(space_real, "scan", split_axis=1, concat_axis=0, tiled=True),
        lax.all_to_all(space_imag, "scan", split_axis=1, concat_axis=0, tiled=True),
    )
    spec_real, spec_imag = pair_left(row_cos, row_sin, whole_real, whole_imag)
    back_real, back_imag = (
        lax.all_to_all(spec_real, "scan", split_axis=0, concat_axis=1, tiled=True),
        lax.all_to_all(spec_imag, "scan", split_axis=0, concat_axis=1, tiled=True),
    )
    block_freqs = back_real.shape[0]
    back_real = back_real.reshape(block_freqs, freq_count, local_rows, detector)
    back_imag = back_imag.reshape(block_freqs, freq_count, local_rows, detector)
    field_real, field_imag = pair_right(
        lax.all_to_all(back_real, "det", split_axis=0, concat_axis=2, tiled=True),
        lax.all_to_all(back_imag, "det", split_axis=0, concat_axis=2, tiled=True),
        "qfay,xa->qfyx",
        inv_cos,
        inv_sin,
    )
    kernel_real = wigner[0]
    kernel_imag = wigner[1]
    power = kernel_real * kernel_real + kernel_imag * kernel_imag + eps_wiener
    filtered_real = (field_real * kernel_real + field_imag * kernel_imag) / power
    filtered_imag = (field_imag * kernel_real - field_real * kernel_imag) / power
    half_real, half_imag = pair_right(
        filtered_real, filtered_imag, "qfyx,ax->qfya", fwd_cos, fwd_sin
    )
    plane_real, plane_imag = pair_right(half_real, half_imag, "qfya,by->qfab", fwd_cos, fwd_sin)
    final_real, final_imag = (
        lax.all_to_all(plane_real, "det", split_axis=2, concat_axis=0, tiled=True),
        lax.all_to_all(plane_imag, "det", split_axis=2, concat_axis=0, tiled=True),
    )
    return jnp.stack([final_real, final_imag])


def solution(mesh):
    in_specs = (P(None, "scan", None, "det", None), P(None, ("scan", "det"), None, None, None))
    out_specs = P(None, "scan", None, "det", None)
    return jax.shard_map(shards, mesh=mesh, in_specs=in_specs, out_specs=out_specs, check_vma=False)
```

profile of v0, /device:TPU:0, one launch (start us, length us, event | category | flops | bytes accessed | tf_op | source)
XLA Modules:
  0.0 1414.9 jit_solution(12617871655616381208)
XLA Ops:
  0.0 6.8 fusion.197
  6.8 20.8 %fusion.6 = f32[256,128,2,32]{1,0,3,2:T(8,128)} fusion(f32[1,128,2,32,256]{4,3,2,1,0:T(8,128)S(1)} %get-tuple-element.8), kind=kOutput, calls=%fused_computation.15 | convolution fusion | flops 6443433984 | bytes 16777216 | tf_op jit(solution)/shard_map/rfab,by->rfay/dot_general | solution.py:20
  27.6 36.1 %fusion.25 = f32[256,128,2,32]{1,0,3,2:T(8,128)} fusion(f32[256,128,2,32]{1,0,3,2:T(8,128)} %fusion.6, f32[1,128,2,32,256]{4,3,2,1,0:T(8,128)S(1)} %get-tuple-element.7), kind=kOutput, calls=%fused_computation.32 | convolution fusion | flops 6445531136 | bytes 25165824 | tf_op jit(solution)/shard_map/rfab,by->rfay/dot_general | solution.py:20
  63.7 9.0 copy.46
  72.7 5.6 all-to-all-start.1
  78.3 23.8 %fusion.7 = f32[256,128,2,32]{1,0,3,2:T(8,128)S(1)} fusion(f32[1,128,2,32,256]{4,3,2,1,0:T(8,128)} %copy-done), kind=kOutput, calls=%fused_computation.16 | convolution fusion | flops 6443433984 | bytes 16777216 | tf_op jit(solution)/shard_map/rfab,by->rfay/dot_general | solution.py:20
  102.1 25.2 %fusion.24 = f32[256,128,2,32]{1,0,3,2:T(8,128)} fusion(f32[256,128,2,32]{1,0,3,2:T(8,128)S(1)} %fusion.7, f32[1,128,2,32,256]{4,3,2,1,0:T(8,128)} %copy-done.3), kind=kOutput, calls=%fused_computation.31 | convolution fusion | flops 6445531136 | bytes 25165824 | tf_op jit(solution)/shard_map/rfab,by->rfay/dot_general | solution.py:20
  127.3 9.0 copy.43
  136.3 35.9 %all-to-all-done.1 = f32[128,4,4096]{2,0,1:T(8,128)} async-done(((f32[128,4,4096]{2,0,1:T(8,128)}), f32[128,4,4096]{2,0,1:T(8,128)}, u32[]{:S(2)}, u32[]{:S(2)}) %all-to-all-start.1) | async-done | bytes 8388640 | tf_op jit(solution)/shard_map/all_to_all | solution.py:53
  172.2 6.1 all-to-all-start
  178.3 25.5 %fusion.32 = f32[512,4096]{1,0:T(8,128)} fusion(f32[512,4096]{1,0:T(8,128)} %bitcast.13), kind=kOutput, calls=%fused_computation.44 | convolution fusion | flops 12888834048 | bytes 16777216 | tf_op jit(solution)/shard_map/dot_general | solution.py:33
  203.8 66.6 %all-to-all-done = f32[128,4,4096]{2,0,1:T(8,128)} async-done(((f32[128,4,4096]{2,0,1:T(8,128)}), f32[128,4,4096]{2,0,1:T(8,128)}, u32[]{:S(2)}, u32[]{:S(2)}) %all-to-all-start) | async-done | bytes 8388640 | tf_op jit(solution)/shard_map/all_to_all | solution.py:52
  270.3 27.0 %convolution_add_fusion = f32[512,4096]{1,0:T(8,128)} fusion(f32[512,4096]{1,0:T(8,128)} %fusion.32, f32[512,4096]{1,0:T(8,128)} %bitcast.7), kind=kOutput, calls=%fused_computation.19 | convolution fusion | flops 12890931200 | bytes 25165824 | tf_op jit(solution)/shard_map/dot_general | solution.py:33
  297.4 8.9 copy.51
  306.3 5.9 all-to-all-start.4
  312.2 23.5 %fusion.33 = f32[512,4096]{1,0:T(8,128)S(1)} fusion(f32[512,4096]{1,0:T(8,128)} %bitcast.7), kind=kOutput, calls=%fused_computation.45 | convolution fusion | flops 12888834048 | bytes 16777216 | tf_op jit(solution)/shard_map/dot_general | solution.py:30
  335.7 26.0 %convolution_subtract_fusion = f32[512,4096]{1,0:T(8,128)} fusion(f32[512,4096]{1,0:T(8,128)S(1)} %fusion.33, f32[512,4096]{1,0:T(8,128)} %bitcast.13), kind=kOutput, calls=%fused_computation.20 | convolution fusion | flops 12890931200 | bytes 25165824 | tf_op jit(solution)/shard_map/dot_general | solution.py:30
  361.7 8.9 copy.47
  370.7 33.3 %all-to-all-done.4 = f32[4,128,4096]{1,2,0:T(8,128)} async-done(((f32[4,128,4096]{1,2,0:T(8,128)}), f32[4,128,4096]{1,2,0:T(8,128)}, u32[]{:S(2)}, u32[]{:S(2)}) %all-to-all-start.4) | async-done | bytes 8388640 | tf_op jit(solution)/shard_map/all_to_all | solution.py:58
  404.0 5.6 all-to-all-start.2
  409.6 10.2 copy.52
  419.8 81.6 %all-to-all-done.2 = f32[4,128,4096]{1,2,0:T(8,128)} async-done(((f32[4,128,4096]{1,2,0:T(8,128)}), f32[4,128,4096]{1,2,0:T(8,128)}, u32[]{:S(2)}, u32[]{:S(2)}) %all-to-all-start.2) | async-done | bytes 8388640 | tf_op jit(solution)/shard_map/all_to_all | solution.py:57
  506.4 10.3 copy.48
  516.7 173.6 %all-to-all-done.5 = f32[128,2,32,256]{3,2,1,0:T(8,128)} async-done(((f32[128,2,32,256]{3,2,1,0:T(8,128)}), f32[128,2,32,256]{3,2,1,0:T(8,128)}, u32[]{:S(2)}, u32[]{:S(2)}) %all-to-all-start.5) | async-done | bytes 8388640 | tf_op jit(solution)/shard_map/all_to_all | solution.py:65
  690.3 5.1 all-to-all-start.3
  699.7 17.8 %fusion.63 = f32[16,2,256,256]{3,2,1,0:T(8,128)} fusion(f32[16,2,256,256]{3,2,1,0:T(8,128)S(1)} %bitcast.141), kind=kOutput, calls=%fused_computation.74 | convolution fusion | flops 6443433984 | bytes 16777216 | tf_op jit(solution)/shard_map/qfay,xa->qfyx/dot_general | solution.py:20
  717.5 17.9 %fusion.53 = f32[16,2,256,256]{3,2,1,0:T(8,128)} fusion(f32[16,2,256,256]{3,2,1,0:T(8,128)S(1)} %bitcast.142), kind=kOutput, calls=%fused_computation.64 | convolution fusion | flops 6443433984 | bytes 16777216 | tf_op jit(solution)/shard_map/qfay,xa->qfyx/dot_general | solution.py:20
  735.5 143.9 %all-to-all-done.3 = f32[128,2,32,256]{3,2,1,0:T(8,128)} async-done(((f32[128,2,32,256]{3,2,1,0:T(8,128)}), f32[128,2,32,256]{3,2,1,0:T(8,128)}, u32[]{:S(2)}, u32[]{:S(2)}) %all-to-all-start.3) | async-done | bytes 8388640 | tf_op jit(solution)/shard_map/all_to_all | solution.py:64
  879.4 5.0 copy.49
  884.4 17.9 %fusion.65 = f32[16,2,256,256]{3,2,1,0:T(8,128)} fusion(f32[16,2,256,256]{3,2,1,0:T(8,128)S(1)} %bitcast.147), kind=kOutput, calls=%fused_computation.76 | convolution fusion | flops 6443433984 | bytes 16777216 | tf_op jit(solution)/shard_map/qfay,xa->qfyx/dot_general | solution.py:20
  902.3 26.3 %fusion.5 = (f32[16,2,256,256]{3,2,1,0:T(8,128)S(1)}, f32[16,2,256,256]{3,2,1,0:T(8,128)}) fusion(f32[2,16,2,256,256]{4,3,2,1,0:T(8,128)} %param.3, f32[16,2,256,256]{3,2,1,0:T(8,128)} %fusion.63, f32[16,2,256,256]{3,2,1,0:T(8,128)} %fusion.65, f32[16,2,256,256]{3,2,1,0:T(8,128)} %fusion.53, f32[16,2,256,256]{3,2,1,0:T(8,128)S(1)} %bitcast.148), kind=kOutput, calls=%fused_computation.11 | convolution fusion | flops 6472794112 | bytes 67108864 | tf_op jit(solution)/shard_map/qfay,xa->qfyx/dot_general | solution.py:20
  928.5 7.7 fusion.58
  936.2 7.9 fusion.49
  944.1 14.1 fusion.47
  958.3 16.0 %fusion.61 = f32[16,2,256,256]{3,2,1,0:T(8,128)} fusion(f32[16,2,256,256]{3,2,1,0:T(8,128)} %get-tuple-element.6), kind=kOutput, calls=%fused_computation.72 | convolution fusion | flops 6443433984 | bytes 16777216 | tf_op jit(solution)/shard_map/qfyx,ax->qfya/dot_general | solution.py:20
  974.3 17.3 %fusion.12 = f32[16,2,256,256]{3,2,1,0:T(8,128)} fusion(f32[16,2,256,256]{3,2,1,0:T(8,128)S(1)} %fusion.47, f32[16,2,256,256]{3,2,1,0:T(8,128)S(1)} %fusion.58), kind=kOutput, calls=%fused_computation.23 | convolution fusion | flops 6445531136 | bytes 25165824 | tf_op jit(solution)/shard_map/qfya,by->qfab/dot_general | solution.py:20
  991.6 20.2 %fusion.18 = f32[16,2,256,256]{3,2,1,0:T(8,128)S(1)} fusion(f32[16,2,256,256]{3,2,1,0:T(8,128)} %fusion.12, f32[16,2,256,256]{3,2,1,0:T(8,128)} %fusion.61, f32[16,2,256,256]{3,2,1,0:T(8,128)S(1)} %fusion.49), kind=kOutput, calls=%fused_computation.29 | convolution fusion | flops 6447628288 | bytes 33554432 | tf_op jit(solution)/shard_map/qfya,by->qfab/dot_general | solution.py:20
  1011.8 10.2 copy.59
  1021.9 5.2 all-to-all-start.6
  1027.1 19.8 %fusion.10 = f32[16,2,256,256]{3,2,1,0:T(8,128)S(1)} fusion(f32[16,2,256,256]{3,2,1,0:T(8,128)} %copy-done.2, f32[16,2,256,256]{3,2,1,0:T(8,128)} %copy-done.1), kind=kOutput, calls=%fused_computation.21 | convolution fusion | flops 6445531136 | bytes 25165824 | tf_op jit(solution)/shard_map/qfya,by->qfab/dot_general | solution.py:20
  1046.9 20.1 %fusion.21 = f32[16,2,256,256]{3,2,1,0:T(8,128)S(1)} fusion(f32[16,2,256,256]{3,2,1,0:T(8,128)S(1)} %fusion.10, f32[16,2,256,256]{3,2,1,0:T(8,128)} %fusion.61, f32[16,2,256,256]{3,2,1,0:T(8,128)} %copy-done.4), kind=kOutput, calls=%fused_computation.30 | convolution fusion | flops 6447628288 | bytes 33554432 | tf_op jit(solution)/shard_map/qfya,by->qfab/dot_general | solution.py:20
  1067.0 10.1 copy.63
  1077.1 133.9 %all-to-all-done.6 = f32[16,2,256,256]{3,1,0,2:T(2,128)} async-done(((f32[16,2,256,256]{3,1,0,2:T(2,128)}), f32[16,2,256,256]{3,1,0,2:T(2,128)}, u32[]{:S(2)}, u32[]{:S(2)}) %all-to-all-start.6) | async-done | bytes 8388640 | tf_op jit(solution)/shard_map/all_to_all | solution.py:80
  1211.0 5.2 all-to-all-start.7
  1216.2 11.4 copy.60
  1227.6 172.5 %all-to-all-done.7 = f32[16,2,256,256]{3,1,0,2:T(2,128)} async-done(((f32[16,2,256,256]{3,1,0,2:T(2,128)}), f32[16,2,256,256]{3,1,0,2:T(2,128)}, u32[]{:S(2)}, u32[]{:S(2)}) %all-to-all-start.7) | async-done | bytes 8388640 | tf_op jit(solution)/shard_map/all_to_all | solution.py:81
  1400.1 8.3 copy.64
  1408.4 6.3 pad_maximum_fusion
  (14 shorter events, 9.3 us)
Async XLA Ops:
  6.8 20.8 %copy-start = (f32[1,128,2,32,256]{4,3,2,1,0:T(8,128)}, f32[1,128,2,32,256]{4,3,2,1,0:T(8,128)S(1)}, u32[]{:S(2)}) copy-start(f32[1,128,2,32,256]{4,3,2,1,0:T(8,128)S(1)} %get-tuple-element.8) | copy-start | bytes 25165828
  6.8 20.8 %copy-start.3 = (f32[1,128,2,32,256]{4,3,2,1,0:T(8,128)}, f32[1,128,2,32,256]{4,3,2,1,0:T(8,128)S(1)}, u32[]{:S(2)}) copy-start(f32[1,128,2,32,256]{4,3,2,1,0:T(8,128)S(1)} %get-tuple-element.7) | copy-start | bytes 25165828
  72.7 99.5 %all-to-all-start.1 = ((f32[128,4,4096]{2,0,1:T(8,128)}), f32[128,4,4096]{2,0,1:T(8,128)}, u32[]{:S(2)}, u32[]{:S(2)}) async-start(f32[128,4,4096]{2,0,1:T(8,128)} %copy.46), calls=%async_computation.1 | async-start | bytes 16777216 | tf_op jit(solution)/shard_map/all_to_all | solution.py:53
  172.2 98.2 %all-to-all-start = ((f32[128,4,4096]{2,0,1:T(8,128)}), f32[128,4,4096]{2,0,1:T(8,128)}, u32[]{:S(2)}, u32[]{:S(2)}) async-start(f32[128,4,4096]{2,0,1:T(8,128)} %copy.43), calls=%async_computation | async-start | bytes 16777216 | tf_op jit(solution)/shard_map/all_to_all | solution.py:52
  306.3 97.7 %all-to-all-start.4 = ((f32[4,128,4096]{1,2,0:T(8,128)}), f32[4,128,4096]{1,2,0:T(8,128)}, u32[]{:S(2)}, u32[]{:S(2)}) async-start(f32[4,128,4096]{1,2,0:T(8,128)} %copy.51), calls=%async_computation.4 | async-start | bytes 16777216 | tf_op jit(solution)/shard_map/all_to_all | solution.py:58
  404.0 97.5 %all-to-all-start.2 = ((f32[4,128,4096]{1,2,0:T(8,128)}), f32[4,128,4096]{1,2,0:T(8,128)}, u32[]{:S(2)}, u32[]{:S(2)}) async-start(f32[4,128,4096]{1,2,0:T(8,128)} %copy.47), calls=%async_computation.2 | async-start | bytes 16777216 | tf_op jit(solution)/shard_map/all_to_all | solution.py:57
  501.5 188.9 %all-to-all-start.5 = ((f32[128,2,32,256]{3,2,1,0:T(8,128)}), f32[128,2,32,256]{3,2,1,0:T(8,128)}, u32[]{:S(2)}, u32[]{:S(2)}) async-start(f32[128,2,32,256]{3,2,1,0:T(8,128)} %copy.52), calls=%async_computation.5 | async-start | bytes 16777216 | tf_op jit(solution)/shard_map/all_to_all | solution.py:65
  690.3 189.0 %all-to-all-start.3 = ((f32[128,2,32,256]{3,2,1,0:T(8,128)}), f32[128,2,32,256]{3,2,1,0:T(8,128)}, u32[]{:S(2)}, u32[]{:S(2)}) async-start(f32[128,2,32,256]{3,2,1,0:T(8,128)} %copy.48), calls=%async_computation.3 | async-start | bytes 16777216 | tf_op jit(solution)/shard_map/all_to_all | solution.py:64
  936.2 38.1 %copy-start.1 = (f32[16,2,256,256]{3,2,1,0:T(8,128)}, f32[16,2,256,256]{3,2,1,0:T(8,128)S(1)}, u32[]{:S(2)}) copy-start(f32[16,2,256,256]{3,2,1,0:T(8,128)S(1)} %fusion.58) | copy-start | bytes 25165828
  944.1 47.5 %copy-start.4 = (f32[16,2,256,256]{3,2,1,0:T(8,128)}, f32[16,2,256,256]{3,2,1,0:T(8,128)S(1)}, u32[]{:S(2)}) copy-start(f32[16,2,256,256]{3,2,1,0:T(8,128)S(1)} %fusion.49) | copy-start | bytes 25165828
  958.2 16.0 %copy-start.2 = (f32[16,2,256,256]{3,2,1,0:T(8,128)}, f32[16,2,256,256]{3,2,1,0:T(8,128)S(1)}, u32[]{:S(2)}) copy-start(f32[16,2,256,256]{3,2,1,0:T(8,128)S(1)} %fusion.47) | copy-start | bytes 25165828
  1021.9 189.1 %all-to-all-start.6 = ((f32[16,2,256,256]{3,1,0,2:T(2,128)}), f32[16,2,256,256]{3,1,0,2:T(2,128)}, u32[]{:S(2)}, u32[]{:S(2)}) async-start(f32[16,2,256,256]{3,1,0,2:T(2,128)} %copy.59), calls=%async_computation.6 | async-start | bytes 16777216 | tf_op jit(solution)/shard_map/all_to_all | solution.py:80
  1211.0 189.1 %all-to-all-start.7 = ((f32[16,2,256,256]{3,1,0,2:T(2,128)}), f32[16,2,256,256]{3,1,0,2:T(2,128)}, u32[]{:S(2)}, u32[]{:S(2)}) async-start(f32[16,2,256,256]{3,1,0,2:T(2,128)} %copy.63), calls=%async_computation.7 | async-start | bytes 16777216 | tf_op jit(solution)/shard_map/all_to_all | solution.py:81
  1400.1 8.3 copy-start.5
where the time goes:
time: 1420 us; the launch traced here: 1410 us
  waiting for transfers between devices  841 us (59%)
  matrix products  411 us (29%)
  local copies, waits for them, and re-layouts  112 us (8%)
  starting transfers between devices  43.7 us (3%)
    dot_general x16, matrix products, product_form(): return jnp.einsum(form, left, right, precision=lax.Precision.HIGHEST)  309 us
    all_to_all x1, waiting for transfers between devices, shards(): lax.all_to_all(back_imag, 'det', split_axis=0, concat_axis=2, tiled=True)  174 us
    all_to_all x1, waiting for transfers between devices, shards(): lax.all_to_all(plane_imag, 'det', split_axis=2, concat_axis=0, tiled=True)  172 us
    all_to_all x1, waiting for transfers between devices, shards(): lax.all_to_all(back_real, 'det', split_axis=0, concat_axis=2, tiled=True)  144 us
    all_to_all x1, waiting for transfers between devices, shards(): lax.all_to_all(plane_real, 'det', split_axis=2, concat_axis=0, tiled=True)  134 us
    all_to_all x1, waiting for transfers between devices, shards(): lax.all_to_all(spec_real, 'scan', split_axis=0, concat_axis=1, tiled=True)  81.6 us
    all_to_all x1, waiting for transfers between devices, shards(): lax.all_to_all(space_real, 'scan', split_axis=1, concat_axis=0, tiled=True)  66.6 us
    all_to_all x1, waiting for transfers between devices, shards(): lax.all_to_all(space_imag, 'scan', split_axis=1, concat_axis=0, tiled=True)  35.9 us
  transfers between devices with their start and end apart: 8, of which 8 were waited for; matrix products, arithmetic and copies ran while one was open for 19% of the time, Pallas kernels for 0%

commit v1 on v0

--- a/solution.py
+++ b/solution.py
@@ -1,8 +1,13 @@
+import functools
 import math
 
 import jax
 import jax.numpy as jnp
+import ml_dtypes
+import numpy as np
 from jax import lax
+from jax.experimental import pallas as pl
+from jax.experimental.pallas import tpu as pltpu
 from jax.sharding import PartitionSpec as P
 
 eps_wiener = 0.1
@@ -36,7 +41,7 @@
     return (real_out, imag_out)
 
 
-def shards(data, wigner):
+def shards_plain(data, wigner):
     detector = data.shape[4]
     freq_count = data.shape[2]
     local_rows = data.shape[3]
@@ -83,7 +88,300 @@
     return jnp.stack([final_real, final_imag])
 
 
+LANES = 128
+PARAMS = pltpu.CompilerParams(vmem_limit_bytes=40 * 1024 * 1024)
+
+
+def phases(left, right, count, sign):
+    angle = 2.0 * math.pi / count * (np.outer(left, right) % count)
+    scale = 1.0 / math.sqrt(count)
+    return np.cos(angle) * scale, sign * np.sin(angle) * scale
+
+
+def halves(table):
+    table = table.astype(np.float32)
+    high = table.astype(ml_dtypes.bfloat16)
+    low = (table - high.astype(np.float32)).astype(ml_dtypes.bfloat16)
+    return jnp.asarray(high), jnp.asarray(low)
+
+
+def right_table(left, right, count, sign):
+    real, imag = phases(left, right, count, sign)
+    return halves(np.block([[real, imag], [-imag, real]]))
+
+
+def split(value):
+    high = value.astype(jnp.bfloat16)
+    low = (value - high.astype(jnp.float32)).astype(jnp.bfloat16)
+    return high, low
+
+
+def dot(left, right):
+    return jnp.dot(left, right, preferred_element_type=jnp.float32)
+
+
+def times(value, high, low):
+    value_high, value_low = split(value)
+    return dot(value_high, high) + (dot(value_low, high) + dot(value_high, low))
+
+
+def column_kernel(me, data, high, low, out):
+    _, rows, _, group, detector = data.shape
+    both = jnp.concatenate(
+        [data[c, :, 0].reshape(rows * group, detector) for c in range(2)], axis=1
+    )
+    result = times(both, high[...], low[...])
+    for c in range(2):
+        part = result[:, c * LANES : (c + 1) * LANES].reshape(rows, group, LANES)
+        out[0, c] = jnp.swapaxes(part, 0, 1)
+
+
+def columns_to_space(me, data, freq, table, parts):
+    _, rows, _, local_rows, detector = data.shape
+    group = local_rows // parts
+    flops = 2 * 3 * rows * local_rows * 2 * detector * 2 * LANES
+    return pl.pallas_call(
+        column_kernel,
+        grid_spec=pltpu.PrefetchScalarGridSpec(
+            num_scalar_prefetch=1,
+            grid=(parts,),
+            in_specs=[
+                pl.BlockSpec(
+                    (2, rows, 1, group, detector),
+                    lambda i, me: (0, 0, freq, jnp.bitwise_xor(i, me[0]), 0),
+                ),
+                pl.BlockSpec((2 * detector, 2 * LANES), lambda i, me: (0, 0)),
+                pl.BlockSpec((2 * detector, 2 * LANES), lambda i, me: (0, 0)),
+            ],
+            out_specs=pl.BlockSpec((1, 2, group, rows, LANES), lambda i, me: (i, 0, 0, 0, 0)),
+        ),
+        out_shape=jax.ShapeDtypeStruct((parts, 2, group, rows, LANES), jnp.float32),
+        compiler_params=PARAMS,
+        cost_estimate=pl.CostEstimate(
+            flops=flops, bytes_accessed=12 * 2 * rows * local_rows * LANES, transcendentals=0
+        ),
+        name="columns_to_space",
+    )(me, data, *table)
+
+
+def row_kernel(me, *refs):
+    sources, (high, low, out, held_high, held_low) = refs[:-5], refs[-5:]
+    parts = len(sources)
+    _, group, rows, _ = sources[0].shape
+    _, block, total = high.shape
+    dests, _, share, _, _ = out.shape
+
+    @pl.when(pl.program_id(0) == 0)
+    def _():
+        for c in range(2):
+            for s in range(parts):
+                sender = jnp.bitwise_xor(me[0], s)
+                at = pl.ds(pl.multiple_of((c * parts + sender) * rows, rows), rows)
+                for a in range(group):
+                    piece_high, piece_low = split(sources[s][c, a])
+                    held_high[at, a * LANES : (a + 1) * LANES] = piece_high
+                    held_low[at, a * LANES : (a + 1) * LANES] = piece_low
+
+    for c in range(2):
+        result = dot(high[c], held_high[...]) + (
+            dot(high[c], held_low[...]) + dot(low[c], held_high[...])
+        )
+        stacked = jnp.stack(
+            [result[:, a * LANES : (a + 1) * LANES] for a in range(group)], axis=1
+        )
+        out[:, c] = stacked.reshape(dests, share, group, LANES)
+
+
+def rows_to_freqs(me, sources, table, devices, steps):
+    parts = len(sources)
+    _, group, rows, _ = sources[0].shape
+    total = parts * rows
+    share = total // devices
+    return pl.pallas_call(
+        row_kernel,
+        grid=(steps,),
+        in_specs=[
+            pl.BlockSpec(memory_space=pltpu.SMEM),
+            *(pl.BlockSpec(source.shape, lambda i: (0, 0, 0, 0)) for source in sources),
+            pl.BlockSpec((2, total // steps, 2 * total), lambda i: (0, i, 0)),
+            pl.BlockSpec((2, total // steps, 2 * total), lambda i: (0, i, 0)),
+        ],
+        out_specs=pl.BlockSpec(
+            (devices // steps, 2, share, group, LANES), lambda i: (i, 0, 0, 0, 0)
+        ),
+        out_shape=jax.ShapeDtypeStruct((devices, 2, share, group, LANES), jnp.float32),
+        scratch_shapes=[pltpu.VMEM((2 * total, group * LANES), jnp.bfloat16)] * 2,
+        compiler_params=PARAMS,
+        cost_estimate=pl.CostEstimate(
+            flops=2 * 3 * 4 * total * total * group * LANES,
+            bytes_accessed=16 * total * group * LANES,
+            transcendentals=0,
+        ),
+        name="rows_to_freqs",
+    )(me, *sources, *table)
+
+
+def filter_kernel(source, wigner, there_high, there_low, back_high, back_low, out):
+    devices, _, batch, group, _ = source.shape
+    dests, _, _, local_rows, _ = out.shape
+    detector = devices * group
+    planes = []
+    for q in range(batch):
+        plane = jnp.concatenate(
+            [source[:, c, q].reshape(detector, LANES) for c in range(2)], axis=0
+        )
+        planes.append(jnp.transpose(plane))
+    field = times(jnp.concatenate(planes, axis=0), there_high[...], there_low[...])
+    field_real, field_imag = field[:, :detector], field[:, detector:]
+    kernel_real = wigner[0, :, 0].reshape(batch * LANES, detector)
+    kernel_imag = wigner[1, :, 0].reshape(batch * LANES, detector)
+    power = kernel_real * kernel_real + kernel_imag * kernel_imag + eps_wiener
+    inverse = 1.0 / power
+    filtered = jnp.concatenate(
+        [
+            (field_real * kernel_real + field_imag * kernel_imag) * inverse,
+            (field_imag * kernel_real - field_real * kernel_imag) * inverse,
+        ],
+        axis=1,
+    )
+    result = times(filtered, back_high[...], back_low[...])
+    for q in range(batch):
+        plane = jnp.transpose(result[q * LANES : (q + 1) * LANES])
+        for c in range(2):
+            part = plane[c * detector : (c + 1) * detector]
+            out[:, c, q] = part.reshape(dests, local_rows, LANES)
+
+
+def filter_planes(source, wigner, freq, chunk, there, back, dests, batch):
+    devices, _, share, group, _ = source.shape
+    detector = devices * group
+    local_rows = detector // dests
+    whole = pl.BlockSpec((2 * detector, 2 * detector), lambda i: (0, 0))
+    return pl.pallas_call(
+        filter_kernel,
+        grid=(share // batch,),
+        in_specs=[
+            pl.BlockSpec((devices, 2, batch, group, LANES), lambda i: (0, 0, i, 0, 0)),
+            pl.BlockSpec((2, batch, 1, LANES, detector), lambda i: (0, i, freq, chunk, 0)),
+            whole,
+            whole,
+            whole,
+            whole,
+        ],
+        out_specs=pl.BlockSpec((dests, 2, batch, local_rows, LANES), lambda i: (0, 0, i, 0, 0)),
+        out_shape=jax.ShapeDtypeStruct((dests, 2, share, local_rows, LANES), jnp.float32),
+        compiler_params=PARAMS,
+        cost_estimate=pl.CostEstimate(
+            flops=2 * 2 * 3 * 4 * share * LANES * detector * detector,
+            bytes_accessed=24 * share * LANES * detector,
+            transcendentals=0,
+        ),
+        name="filter_planes",
+    )(source, wigner, *there, *back)
+
+
+def final_kernel(*refs):
+    sources, (high, low), out = refs[:-3], refs[-3:-1], refs[-1]
+    _, _, share, local_rows, _ = sources[0].shape
+    detector = out.shape[4]
+    rows = share * local_rows
+    both = jnp.concatenate(
+        [piece[0, c].reshape(rows, LANES) for c in range(2) for piece in sources], axis=1
+    )
+    result = times(both, high[...], low[...])
+    for c in range(2):
+        part = result[:, c * detector : (c + 1) * detector]
+        out[c, :, 0] = part.reshape(share, local_rows, detector)
+
+
+def space_to_columns(sources, freq, freq_count, table, held):
+    dests, _, share, local_rows, _ = sources[0].shape
+    detector = len(sources) * LANES
+    whole = pl.BlockSpec((2 * detector, 2 * detector), lambda i: (0, 0))
+    in_specs = [
+        pl.BlockSpec((1, 2, share, local_rows, LANES), lambda i: (i, 0, 0, 0, 0)) for _ in sources
+    ] + [whole, whole]
+    args = list(sources) + list(table)
+    body = final_kernel
+    aliases = {}
+    if held is not None:
+        in_specs = [pl.BlockSpec(memory_space=pl.ANY)] + in_specs
+        args = [held] + args
+        aliases = {0: 0}
+        body = lambda *refs: final_kernel(*refs[1:])
+    return pl.pallas_call(
+        body,
+        grid=(dests,),
+        in_specs=in_specs,
+        out_specs=pl.BlockSpec((2, share, 1, local_rows, detector), lambda i: (0, i, freq, 0, 0)),
+        out_shape=jax.ShapeDtypeStruct(
+            (2, dests * share, freq_count, local_rows, detector), jnp.float32
+        ),
+        input_output_aliases=aliases,
+        compiler_params=PARAMS,
+        cost_estimate=pl.CostEstimate(
+            flops=2 * 3 * 4 * dests * share * local_rows * detector * detector,
+            bytes_accessed=16 * dests * share * local_rows * detector,
+            transcendentals=0,
+        ),
+        name="space_to_columns",
+    )(*args)
+
+
+def shards(data, wigner, scan, det):
+    _, rows, freq_count, local_rows, detector = data.shape
+    devices = scan * det
+    group = local_rows // scan
+    total = rows * scan
+    points = np.arange(detector)
+    chunks = detector // LANES
+    spaces = [
+        right_table(points, points[k * LANES : (k + 1) * LANES], detector, 1.0)
+        for k in range(chunks)
+    ]
+    real, imag = phases(np.arange(total), np.arange(total), total, -1.0)
+    row_table = tuple(
+        part.reshape(2, total, 2 * total)
+        for part in halves(np.block([[real, -imag], [imag, real]]))
+    )
+    arrival = points.reshape(det, scan, group).transpose(1, 0, 2).reshape(-1)
+    there = right_table(arrival, points, detector, 1.0)
+    back = right_table(points, points, detector, -1.0)
+
+    me = lax.axis_index("scan").astype(jnp.int32).reshape(1)
+    turn = me
+    out = None
+    for freq in range(freq_count):
+        pieces = []
+        for k in range(chunks):
+            space = columns_to_space(turn, data, freq, spaces[k], scan)
+            sources = [space[0]] + [
+                lax.ppermute(space[i], "scan", [(j, j ^ i) for j in range(scan)])
+                for i in range(1, scan)
+            ]
+            turn, sources = lax.optimization_barrier((turn, sources))
+            spec = rows_to_freqs(me, sources, row_table, devices, scan)
+            spec = lax.all_to_all(
+                spec, ("scan", "det"), split_axis=0, concat_axis=0, tiled=True
+            )
+            plane = filter_planes(spec, wigner, freq, k, there, back, det, 2)
+            pieces.append(lax.all_to_all(plane, "det", split_axis=0, concat_axis=0, tiled=True))
+        out = space_to_columns(pieces, freq, freq_count, back, out)
+    return out
+
+
 def solution(mesh):
     in_specs = (P(None, "scan", None, "det", None), P(None, ("scan", "det"), None, None, None))
     out_specs = P(None, "scan", None, "det", None)
-    return jax.shard_map(shards, mesh=mesh, in_specs=in_specs, out_specs=out_specs, check_vma=False)
+    scan, det = mesh.shape["scan"], mesh.shape["det"]
+
+    def whole(data, wigner):
+        detector = data.shape[4]
+        share = data.shape[1] // (scan * det)
+        tiled = detector % max(8 * scan * det, LANES) == 0 and share % 2 == 0 and scan & (scan - 1) == 0
+        body = functools.partial(shards, scan=scan, det=det) if tiled else shards_plain
+        return jax.shard_map(
+            body, mesh=mesh, in_specs=in_specs, out_specs=out_specs, check_vma=False
+        )(data, wigner)
+
+    return whole

time: 1420 us -> 932 us (0.66)
  matrix products: 411 us -> 0 us
  Pallas kernels: 0 us -> 143 us
  waiting for transfers between devices: 841 us -> 716 us
  local copies, waits for them, and re-layouts: 112 us -> 19.9 us
    all_to_all x8, waiting for transfers between devices: 841 us -> 404 us  [the longest x4 323 us: shards(): lax.all_to_all(plane, 'det', split_axis=0, concat_axis=0, tiled=True)]
    dot_general x20 -> x0, matrix products: 411 us -> none  [the longest x16 309 us: product_form(): return jnp.einsum(form, left, right, precision=lax.Precision.HIGHEST)]
    ppermute x0 -> x12, waiting for transfers between devices: none -> 312 us  [shards(): lax.ppermute(space[i], 'scan', [(j, j ^ i) for j in range(scan)])]
    pallas_call x0 -> x14, Pallas kernels: none -> 143 us  [the longest x4 46.8 us: filter_planes(): pl.pallas_call(filter_kernel, grid=(share // batch,), in_specs=[pl.BlockS...]
    all_to_all x8 -> x0, local copies, waits for them, and re-layouts: 64.8 us -> none  [the longest x1 11.4 us: shards(): lax.all_to_all(plane_real, 'det', split_axis=2, concat_axis=0, tiled=True)]
    reshape x2 -> x0, local copies, waits for them, and re-layouts: 20.5 us -> none  [the longest x1 10.3 us: shards(): back_real = back_real.reshape(block_freqs, freq_count, local_rows, detector)]
    unnamed x12 -> x46, local copies, waits for them, and re-layouts: 0.02 us -> 17.9 us
    ppermute x0 -> x12, starting transfers between devices: none -> 15.3 us  [shards(): lax.ppermute(space[i], 'scan', [(j, j ^ i) for j in range(scan)])]
  transfers between devices with their start and end apart: 8 -> 20, of which waited for: 8 -> 17; matrix products, arithmetic and copies ran while one was open for 19% -> 0% of each run, Pallas kernels for 0% -> 12%
where the time goes in v1:
time: 932 us; the launch traced here: 931 us
  waiting for transfers between devices  716 us (77%)
  Pallas kernels  143 us (15%)
  starting transfers between devices  51.1 us (5%)
  local copies, waits for them, and re-layouts  19.9 us (2%)
    all_to_all x4, waiting for transfers between devices, shards(): lax.all_to_all(plane, 'det', split_axis=0, concat_axis=0, tiled=True)  323 us
    ppermute x12, waiting for transfers between devices, shards(): lax.ppermute(space[i], 'scan', [(j, j ^ i) for j in range(scan)])  312 us
    all_to_all x4, waiting for transfers between devices, shards(): lax.all_to_all(spec, ('scan', 'det'), split_axis=0, concat_axis=0, tiled=...  81.3 us
    pallas_call x4, Pallas kernels, filter_planes(): pl.pallas_call(filter_kernel, grid=(share // batch,), in_specs=[pl.BlockS...  46.8 us
    pallas_call x4, Pallas kernels, rows_to_freqs(): pl.pallas_call(row_kernel, grid=(steps,), in_specs=[pl.BlockSpec(memory_s...  46.5 us
    pallas_call x4, Pallas kernels, columns_to_space(): pl.pallas_call(column_kernel, grid_spec=pltpu.PrefetchScalarGridSpec(num_...  25.8 us
    pallas_call x2, Pallas kernels, space_to_columns(): pl.pallas_call(body, grid=(dests,), in_specs=in_specs, out_specs=pl.Block...  24.2 us
  transfers between devices with their start and end apart: 20, of which 17 were waited for; matrix products, arithmetic and copies ran while one was open for 0% of the time, Pallas kernels for 12%

profile of v1, /device:TPU:0, one launch (start us, length us, event | category | flops | bytes accessed | tf_op | source)
XLA Modules:
  0.0 931.0 jit_solution(806271808415217868)
XLA Ops:
  1.9 6.4 columns_to_space.4
  8.9 4.0 collective-permute-start.2
  13.5 23.4 %collective-permute-done.2.refs_3_ = f32[2,8,128,128]{3,2,1,0:T(8,128)S(1)} collective-permute-done((f32[2,8,128,128]{3,2,1,0:T(8,128)S(1)}, f32[2,8,128,128]{3,2,1,0:T(8,128)S(1)}, u32[]{:S(2)}, u32[]{:S(2)}) %collective-permute-start.2) | collective-permute-done | bytes 1048608 | tf_op jit(solution)/shard_map/ppermute | solution.py:359
  36.9 21.6 %collective-permute-done.1.refs_2_ = f32[2,8,128,128]{3,2,1,0:T(8,128)S(1)} collective-permute-done((f32[2,8,128,128]{3,2,1,0:T(8,128)S(1)}, f32[2,8,128,128]{3,2,1,0:T(8,128)S(1)}, u32[]{:S(2)}, u32[]{:S(2)}) %collective-permute-start.1) | collective-permute-done | bytes 1048608 | tf_op jit(solution)/shard_map/ppermute | solution.py:359
  58.7 11.6 %rows_to_freqs.4 = f32[32,2,16,8,128]{4,3,2,1,0:T(8,128)S(1)} custom-call(s32[1]{0:T(128)} %bitcast.me, f32[2,8,128,128]{3,2,1,0:T(8,128)S(1)} %get-tuple-element.24.refs_0_, f32[2,8,128,128]{3,2,1,0:T(8,128)S(1)} %collective-permute-done.refs_1_, f32[2,8,128,128]{3,2,1,0:T(8,128)S(1)} %collective-permute-done.1.refs_2_, ...), custom_call_target="tpu_custom_call" | custom-call | flops 6442450944 | bytes 8388608 | tf_op jit(solution)/shard_map/rows_to_freqs/pallas_call | solution.py:200
  70.4 2.0 copy-done.10
  72.4 5.2 all-to-all-start
  77.6 6.4 columns_to_space.5
  84.6 2.7 collective-permute-start.5
  88.2 59.6 %collective-permute-done.5.refs_3_ = f32[2,8,128,128]{3,2,1,0:T(8,128)S(1)} collective-permute-done((f32[2,8,128,128]{3,2,1,0:T(8,128)S(1)}, f32[2,8,128,128]{3,2,1,0:T(8,128)S(1)}, u32[]{:S(2)}, u32[]{:S(2)}) %collective-permute-start.5) | collective-permute-done | bytes 1048608 | tf_op jit(solution)/shard_map/ppermute | solution.py:359
  147.8 19.7 %collective-permute-done.4.refs_2_ = f32[2,8,128,128]{3,2,1,0:T(8,128)S(1)} collective-permute-done((f32[2,8,128,128]{3,2,1,0:T(8,128)S(1)}, f32[2,8,128,128]{3,2,1,0:T(8,128)S(1)}, u32[]{:S(2)}, u32[]{:S(2)}) %collective-permute-start.4) | collective-permute-done | bytes 1048608 | tf_op jit(solution)/shard_map/ppermute | solution.py:359
  167.4 9.7 %collective-permute-done.3.refs_1_ = f32[2,8,128,128]{3,2,1,0:T(8,128)S(1)} collective-permute-done((f32[2,8,128,128]{3,2,1,0:T(8,128)S(1)}, f32[2,8,128,128]{3,2,1,0:T(8,128)S(1)}, u32[]{:S(2)}, u32[]{:S(2)}) %collective-permute-start.3) | collective-permute-done | bytes 1048608 | tf_op jit(solution)/shard_map/ppermute | solution.py:359
  177.2 11.6 %rows_to_freqs.5 = f32[32,2,16,8,128]{4,3,2,1,0:T(8,128)S(1)} custom-call(s32[1]{0:T(128)} %bitcast.me, f32[2,8,128,128]{3,2,1,0:T(8,128)S(1)} %get-tuple-element.29.refs_0_, f32[2,8,128,128]{3,2,1,0:T(8,128)S(1)} %collective-permute-done.3.refs_1_, f32[2,8,128,128]{3,2,1,0:T(8,128)S(1)} %collective-permute-done.4.refs_2_, ...), custom_call_target="tpu_custom_call" | custom-call | flops 6442450944 | bytes 8388608 | tf_op jit(solution)/shard_map/rows_to_freqs/pallas_call | solution.py:200
  188.8 2.0 copy-done.9
  190.9 4.2 all-to-all-start.2
  195.1 6.4 columns_to_space.6
  202.0 2.5 collective-permute-start.8
  205.6 59.4 %collective-permute-done.8.refs_3_ = f32[2,8,128,128]{3,2,1,0:T(8,128)S(1)} collective-permute-done((f32[2,8,128,128]{3,2,1,0:T(8,128)S(1)}, f32[2,8,128,128]{3,2,1,0:T(8,128)S(1)}, u32[]{:S(2)}, u32[]{:S(2)}) %collective-permute-start.8) | collective-permute-done | bytes 1048608 | tf_op jit(solution)/shard_map/ppermute | solution.py:359
  265.0 19.7 %collective-permute-done.7.refs_2_ = f32[2,8,128,128]{3,2,1,0:T(8,128)S(1)} collective-permute-done((f32[2,8,128,128]{3,2,1,0:T(8,128)S(1)}, f32[2,8,128,128]{3,2,1,0:T(8,128)S(1)}, u32[]{:S(2)}, u32[]{:S(2)}) %collective-permute-start.7) | collective-permute-done | bytes 1048608 | tf_op jit(solution)/shard_map/ppermute | solution.py:359
  284.7 9.7 %collective-permute-done.6.refs_1_ = f32[2,8,128,128]{3,2,1,0:T(8,128)S(1)} collective-permute-done((f32[2,8,128,128]{3,2,1,0:T(8,128)S(1)}, f32[2,8,128,128]{3,2,1,0:T(8,128)S(1)}, u32[]{:S(2)}, u32[]{:S(2)}) %collective-permute-start.6) | collective-permute-done | bytes 1048608 | tf_op jit(solution)/shard_map/ppermute | solution.py:359
  294.4 11.6 %rows_to_freqs.6 = f32[32,2,16,8,128]{4,3,2,1,0:T(8,128)S(1)} custom-call(s32[1]{0:T(128)} %bitcast.me, f32[2,8,128,128]{3,2,1,0:T(8,128)S(1)} %get-tuple-element.34.refs_0_, f32[2,8,128,128]{3,2,1,0:T(8,128)S(1)} %collective-permute-done.6.refs_1_, f32[2,8,128,128]{3,2,1,0:T(8,128)S(1)} %collective-permute-done.7.refs_2_, ...), custom_call_target="tpu_custom_call" | custom-call | flops 6442450944 | bytes 8388608 | tf_op jit(solution)/shard_map/rows_to_freqs/pallas_call | solution.py:200
  306.1 2.0 copy-done.8
  308.1 4.0 all-to-all-start.4
  312.1 6.4 columns_to_space.7
  319.1 2.7 collective-permute-start.11
  322.6 59.6 %collective-permute-done.11.refs_3_ = f32[2,8,128,128]{3,2,1,0:T(8,128)S(1)} collective-permute-done((f32[2,8,128,128]{3,2,1,0:T(8,128)S(1)}, f32[2,8,128,128]{3,2,1,0:T(8,128)S(1)}, u32[]{:S(2)}, u32[]{:S(2)}) %collective-permute-start.11) | collective-permute-done | bytes 1048608 | tf_op jit(solution)/shard_map/ppermute | solution.py:359
  382.3 19.7 %collective-permute-done.10.refs_2_ = f32[2,8,128,128]{3,2,1,0:T(8,128)S(1)} collective-permute-done((f32[2,8,128,128]{3,2,1,0:T(8,128)S(1)}, f32[2,8,128,128]{3,2,1,0:T(8,128)S(1)}, u32[]{:S(2)}, u32[]{:S(2)}) %collective-permute-start.10) | collective-permute-done | bytes 1048608 | tf_op jit(solution)/shard_map/ppermute | solution.py:359
  401.9 9.7 %collective-permute-done.9.refs_1_ = f32[2,8,128,128]{3,2,1,0:T(8,128)S(1)} collective-permute-done((f32[2,8,128,128]{3,2,1,0:T(8,128)S(1)}, f32[2,8,128,128]{3,2,1,0:T(8,128)S(1)}, u32[]{:S(2)}, u32[]{:S(2)}) %collective-permute-start.9) | collective-permute-done | bytes 1048608 | tf_op jit(solution)/shard_map/ppermute | solution.py:359
  411.7 11.6 %rows_to_freqs.7 = f32[32,2,16,8,128]{4,3,2,1,0:T(8,128)S(1)} custom-call(s32[1]{0:T(128)} %bitcast.me, f32[2,8,128,128]{3,2,1,0:T(8,128)S(1)} %get-tuple-element.39.refs_0_, f32[2,8,128,128]{3,2,1,0:T(8,128)S(1)} %collective-permute-done.9.refs_1_, f32[2,8,128,128]{3,2,1,0:T(8,128)S(1)} %collective-permute-done.10.refs_2_, ...), custom_call_target="tpu_custom_call" | custom-call | flops 6442450944 | bytes 8388608 | tf_op jit(solution)/shard_map/rows_to_freqs/pallas_call | solution.py:200
  423.3 2.0 copy-done.11
  425.3 4.0 all-to-all-start.6
  429.4 11.7 %filter_planes.4 = f32[8,2,16,32,128]{4,3,2,1,0:T(8,128)S(1)} custom-call(f32[32,2,16,8,128]{4,3,2,1,0:T(8,128)} %all-to-all-done.source, f32[2,16,2,256,256]{4,3,2,1,0:T(8,128)} %wigner.7, bf16[512,512]{1,0:T(8,128)(2,1)S(1)} %copy-done.7, bf16[512,512]{1,0:T(8,128)(2,1)S(1)} %copy-done.6, bf16[512,512]{1,0:T(8,128)(2,1)S(1)} %copy-done.1, ...), custom_call_target="tpu_custom_call" | custom-call | flops 6442450944 | bytes 12582912 | tf_op jit(solution)/shard_map/filter_planes/pallas_call | solution.py:260
  441.1 2.0 copy-done.4
  443.1 81.3 %all-to-all-done.6.source = f32[32,2,16,8,128]{4,3,2,1,0:T(8,128)} async-done(((f32[32,2,16,8,128]{4,3,2,1,0:T(8,128)}), f32[32,2,16,8,128]{4,3,2,1,0:T(8,128)}, u32[]{:S(2)}, u32[]{:S(2)}) %all-to-all-start.6) | async-done | bytes 4194336 | tf_op jit(solution)/shard_map/all_to_all | solution.py:364
  524.4 4.6 all-to-all-start.1
  529.0 11.7 %filter_planes.5 = f32[8,2,16,32,128]{4,3,2,1,0:T(8,128)S(1)} custom-call(f32[32,2,16,8,128]{4,3,2,1,0:T(8,128)} %all-to-all-done.2.source, f32[2,16,2,256,256]{4,3,2,1,0:T(8,128)} %wigner.7, bf16[512,512]{1,0:T(8,128)(2,1)S(1)} %copy-done.7, bf16[512,512]{1,0:T(8,128)(2,1)S(1)} %copy-done.6, bf16[512,512]{1,0:T(8,128)(2,1)S(1)} %copy-done.1, ...), custom_call_target="tpu_custom_call" | custom-call | flops 6442450944 | bytes 12582912 | tf_op jit(solution)/shard_map/filter_planes/pallas_call | solution.py:260
  542.7 80.3 %all-to-all-done.1.refs_0_ = f32[8,2,16,32,128]{4,3,2,1,0:T(8,128)} async-done(((f32[8,2,16,32,128]{4,3,2,1,0:T(8,128)}), f32[8,2,16,32,128]{4,3,2,1,0:T(8,128)}, u32[]{:S(2)}, u32[]{:S(2)}) %all-to-all-start.1) | async-done | bytes 4194336 | tf_op jit(solution)/shard_map/all_to_all | solution.py:368
  623.0 4.8 all-to-all-start.3
  627.7 11.7 %filter_planes.6 = f32[8,2,16,32,128]{4,3,2,1,0:T(8,128)S(1)} custom-call(f32[32,2,16,8,128]{4,3,2,1,0:T(8,128)} %all-to-all-done.4.source, f32[2,16,2,256,256]{4,3,2,1,0:T(8,128)} %wigner.7, bf16[512,512]{1,0:T(8,128)(2,1)S(1)} %copy-done.7, bf16[512,512]{1,0:T(8,128)(2,1)S(1)} %copy-done.6, bf16[512,512]{1,0:T(8,128)(2,1)S(1)} %copy-done.1, ...), custom_call_target="tpu_custom_call" | custom-call | flops 6442450944 | bytes 12582912 | tf_op jit(solution)/shard_map/filter_planes/pallas_call | solution.py:260
  639.5 2.0 copy-done.3
  641.5 80.3 %all-to-all-done.3.refs_1_ = f32[8,2,16,32,128]{4,3,2,1,0:T(8,128)} async-done(((f32[8,2,16,32,128]{4,3,2,1,0:T(8,128)}), f32[8,2,16,32,128]{4,3,2,1,0:T(8,128)}, u32[]{:S(2)}, u32[]{:S(2)}) %all-to-all-start.3) | async-done | bytes 4194336 | tf_op jit(solution)/shard_map/all_to_all | solution.py:368
  721.8 4.5 all-to-all-start.5
  726.3 11.7 %filter_planes.7 = f32[8,2,16,32,128]{4,3,2,1,0:T(8,128)S(1)} custom-call(f32[32,2,16,8,128]{4,3,2,1,0:T(8,128)} %all-to-all-done.6.source, f32[2,16,2,256,256]{4,3,2,1,0:T(8,128)} %wigner.7, bf16[512,512]{1,0:T(8,128)(2,1)S(1)} %copy-done.7, bf16[512,512]{1,0:T(8,128)(2,1)S(1)} %copy-done.6, bf16[512,512]{1,0:T(8,128)(2,1)S(1)} %copy-done.1, ...), custom_call_target="tpu_custom_call" | custom-call | flops 6442450944 | bytes 12582912 | tf_op jit(solution)/shard_map/filter_planes/pallas_call | solution.py:260
  740.0 80.3 %all-to-all-done.5.refs_1_ = f32[8,2,16,32,128]{4,3,2,1,0:T(8,128)} async-done(((f32[8,2,16,32,128]{4,3,2,1,0:T(8,128)}), f32[8,2,16,32,128]{4,3,2,1,0:T(8,128)}, u32[]{:S(2)}, u32[]{:S(2)}) %all-to-all-start.5) | async-done | bytes 4194336 | tf_op jit(solution)/shard_map/all_to_all | solution.py:368
  820.3 4.6 all-to-all-start.7
  824.9 12.1 %space_to_columns.2.refs_0_ = f32[2,128,2,32,256]{4,3,2,1,0:T(8,128)} custom-call(f32[8,2,16,32,128]{4,3,2,1,0:T(8,128)} %all-to-all-done.1.refs_0_, f32[8,2,16,32,128]{4,3,2,1,0:T(8,128)} %all-to-all-done.3.refs_1_, bf16[512,512]{1,0:T(8,128)(2,1)S(1)} %copy-done.1, bf16[512,512]{1,0:T(8,128)(2,1)S(1)} %copy-done), custom_call_target="tpu_custom_call" | custom-call | flops 6442450944 | bytes 16777216 | tf_op jit(solution)/shard_map/space_to_columns/pallas_call | solution.py:312
  837.0 81.9 %all-to-all-done.7.refs_2_ = f32[8,2,16,32,128]{4,3,2,1,0:T(8,128)} async-done(((f32[8,2,16,32,128]{4,3,2,1,0:T(8,128)}), f32[8,2,16,32,128]{4,3,2,1,0:T(8,128)}, u32[]{:S(2)}, u32[]{:S(2)}) %all-to-all-start.7) | async-done | bytes 4194336 | tf_op jit(solution)/shard_map/all_to_all | solution.py:368
  918.9 12.1 %space_to_columns.3 = f32[2,128,2,32,256]{4,3,2,1,0:T(8,128)} custom-call(f32[2,128,2,32,256]{4,3,2,1,0:T(8,128)} %space_to_columns.2.refs_0_, f32[8,2,16,32,128]{4,3,2,1,0:T(8,128)} %all-to-all-done.5.refs_1_, f32[8,2,16,32,128]{4,3,2,1,0:T(8,128)} %all-to-all-done.7.refs_2_, bf16[512,512]{1,0:T(8,128)(2,1)S(1)} %copy-done.1, ...), custom_call_target="tpu_custom_call", output_to_operand_aliasing={{}: (0, {})} | custom-call | flops 6442450944 | bytes 16777216 | tf_op jit(solution)/shard_map/space_to_columns/pallas_call | solution.py:312
  (56 shorter events, 11.7 us)
Async XLA Ops:
  0.0 0.9 copy-start.14
  1.0 0.9 copy-start.16
  8.3 50.4 %copy-start.18 = (bf16[2,512,1024]{2,1,0:T(8,128)(2,1)S(1)}, bf16[2,512,1024]{2,1,0:T(8,128)(2,1)}, u32[]{:S(2)}) copy-start(bf16[2,512,1024]{2,1,0:T(8,128)(2,1)} %constant.37.refs_5_) | copy-start | bytes 6291460
  8.4 50.4 %copy-start.19 = (bf16[2,512,1024]{2,1,0:T(8,128)(2,1)S(1)}, bf16[2,512,1024]{2,1,0:T(8,128)(2,1)}, u32[]{:S(2)}) copy-start(bf16[2,512,1024]{2,1,0:T(8,128)(2,1)} %constant.36.refs_4_) | copy-start | bytes 6291460
  8.9 28.0 %collective-permute-start.2 = (f32[2,8,128,128]{3,2,1,0:T(8,128)S(1)}, f32[2,8,128,128]{3,2,1,0:T(8,128)S(1)}, u32[]{:S(2)}, u32[]{:S(2)}) collective-permute-start(f32[2,8,128,128]{3,2,1,0:T(8,128)S(1)} %get-tuple-element.55), channel_id=1, source_target_pairs={{0,24},{8,16},{16,8},{24,0},{1,25},{9,17},{17,9},{25,1},{2,26},{10... | collective-permute-start | bytes 3145736 | tf_op jit(solution)/shard_map/ppermute | solution.py:359
  12.8 45.6 %collective-permute-start.1 = (f32[2,8,128,128]{3,2,1,0:T(8,128)S(1)}, f32[2,8,128,128]{3,2,1,0:T(8,128)S(1)}, u32[]{:S(2)}, u32[]{:S(2)}) collective-permute-start(f32[2,8,128,128]{3,2,1,0:T(8,128)S(1)} %get-tuple-element.56), channel_id=1, source_target_pairs={{0,16},{8,24},{16,0},{24,8},{1,17},{9,25},{17,1},{25,9},{2,18},{10... | collective-permute-start | bytes 3145736 | tf_op jit(solution)/shard_map/ppermute | solution.py:359
  13.3 45.4 %collective-permute-start = (f32[2,8,128,128]{3,2,1,0:T(8,128)S(1)}, f32[2,8,128,128]{3,2,1,0:T(8,128)S(1)}, u32[]{:S(2)}, u32[]{:S(2)}) collective-permute-start(f32[2,8,128,128]{3,2,1,0:T(8,128)S(1)} %get-tuple-element.57), channel_id=1, source_target_pairs={{0,8},{8,0},{16,24},{24,16},{1,9},{9,1},{17,25},{25,17},{2,10},{10... | collective-permute-start | bytes 3145736 | tf_op jit(solution)/shard_map/ppermute | solution.py:359
  70.4 2.0 copy-start.10
  72.4 5.2 copy-start.12
  72.4 5.2 copy-start.13
  72.4 118.5 %all-to-all-start = ((f32[32,2,16,8,128]{4,3,2,1,0:T(8,128)}), f32[32,2,16,8,128]{4,3,2,1,0:T(8,128)}, u32[]{:S(2)}, u32[]{:S(2)}) async-start(f32[32,2,16,8,128]{4,3,2,1,0:T(8,128)} %copy-done.10), calls=%async_computation | async-start | bytes 8388608 | tf_op jit(solution)/shard_map/all_to_all | solution.py:364
  84.1 93.1 %copy-start.20 = (bf16[2,512,1024]{2,1,0:T(8,128)(2,1)S(1)}, bf16[2,512,1024]{2,1,0:T(8,128)(2,1)}, u32[]{:S(2)}) copy-start(bf16[2,512,1024]{2,1,0:T(8,128)(2,1)} %constant.36.refs_4_) | copy-start | bytes 6291460
  84.6 63.2 %collective-permute-start.5 = (f32[2,8,128,128]{3,2,1,0:T(8,128)S(1)}, f32[2,8,128,128]{3,2,1,0:T(8,128)S(1)}, u32[]{:S(2)}, u32[]{:S(2)}) collective-permute-start(f32[2,8,128,128]{3,2,1,0:T(8,128)S(1)} %get-tuple-element.51), channel_id=1, source_target_pairs={{0,24},{8,16},{16,8},{24,0},{1,25},{9,17},{17,9},{25,1},{2,26},{10... | collective-permute-start | bytes 3145736 | tf_op jit(solution)/shard_map/ppermute | solution.py:359
  87.3 80.2 %collective-permute-start.4 = (f32[2,8,128,128]{3,2,1,0:T(8,128)S(1)}, f32[2,8,128,128]{3,2,1,0:T(8,128)S(1)}, u32[]{:S(2)}, u32[]{:S(2)}) collective-permute-start(f32[2,8,128,128]{3,2,1,0:T(8,128)S(1)} %get-tuple-element.52), channel_id=1, source_target_pairs={{0,16},{8,24},{16,0},{24,8},{1,17},{9,25},{17,1},{25,9},{2,18},{10... | collective-permute-start | bytes 3145736 | tf_op jit(solution)/shard_map/ppermute | solution.py:359
  87.8 89.4 %collective-permute-start.3 = (f32[2,8,128,128]{3,2,1,0:T(8,128)S(1)}, f32[2,8,128,128]{3,2,1,0:T(8,128)S(1)}, u32[]{:S(2)}, u32[]{:S(2)}) collective-permute-start(f32[2,8,128,128]{3,2,1,0:T(8,128)S(1)} %get-tuple-element.53), channel_id=1, source_target_pairs={{0,8},{8,0},{16,24},{24,16},{1,9},{9,1},{17,25},{25,17},{2,10},{10... | collective-permute-start | bytes 3145736 | tf_op jit(solution)/shard_map/ppermute | solution.py:359
  188.8 2.0 copy-start.9
  190.8 4.2 copy-start.15
  190.9 4.2 copy-start.17
  190.9 117.2 %all-to-all-start.2 = ((f32[32,2,16,8,128]{4,3,2,1,0:T(8,128)}), f32[32,2,16,8,128]{4,3,2,1,0:T(8,128)}, u32[]{:S(2)}, u32[]{:S(2)}) async-start(f32[32,2,16,8,128]{4,3,2,1,0:T(8,128)} %copy-done.9), calls=%async_computation.2 | async-start | bytes 8388608 | tf_op jit(solution)/shard_map/all_to_all | solution.py:364
  201.5 92.9 %copy-start.21 = (bf16[2,512,1024]{2,1,0:T(8,128)(2,1)S(1)}, bf16[2,512,1024]{2,1,0:T(8,128)(2,1)}, u32[]{:S(2)}) copy-start(bf16[2,512,1024]{2,1,0:T(8,128)(2,1)} %constant.36.refs_4_) | copy-start | bytes 6291460
  202.0 63.0 %collective-permute-start.8 = (f32[2,8,128,128]{3,2,1,0:T(8,128)S(1)}, f32[2,8,128,128]{3,2,1,0:T(8,128)S(1)}, u32[]{:S(2)}, u32[]{:S(2)}) collective-permute-start(f32[2,8,128,128]{3,2,1,0:T(8,128)S(1)} %get-tuple-element.47), channel_id=1, source_target_pairs={{0,24},{8,16},{16,8},{24,0},{1,25},{9,17},{17,9},{25,1},{2,26},{10... | collective-permute-start | bytes 3145736 | tf_op jit(solution)/shard_map/ppermute | solution.py:359
  204.5 80.2 %collective-permute-start.7 = (f32[2,8,128,128]{3,2,1,0:T(8,128)S(1)}, f32[2,8,128,128]{3,2,1,0:T(8,128)S(1)}, u32[]{:S(2)}, u32[]{:S(2)}) collective-permute-start(f32[2,8,128,128]{3,2,1,0:T(8,128)S(1)} %get-tuple-element.48), channel_id=1, source_target_pairs={{0,16},{8,24},{16,0},{24,8},{1,17},{9,25},{17,1},{25,9},{2,18},{10... | collective-permute-start | bytes 3145736 | tf_op jit(solution)/shard_map/ppermute | solution.py:359
  205.1 89.3 %collective-permute-start.6 = (f32[2,8,128,128]{3,2,1,0:T(8,128)S(1)}, f32[2,8,128,128]{3,2,1,0:T(8,128)S(1)}, u32[]{:S(2)}, u32[]{:S(2)}) collective-permute-start(f32[2,8,128,128]{3,2,1,0:T(8,128)S(1)} %get-tuple-element.49), channel_id=1, source_target_pairs={{0,8},{8,0},{16,24},{24,16},{1,9},{9,1},{17,25},{25,17},{2,10},{10... | collective-permute-start | bytes 3145736 | tf_op jit(solution)/shard_map/ppermute | solution.py:359
  306.1 2.0 copy-start.8
  308.1 117.2 %all-to-all-start.4 = ((f32[32,2,16,8,128]{4,3,2,1,0:T(8,128)}), f32[32,2,16,8,128]{4,3,2,1,0:T(8,128)}, u32[]{:S(2)}, u32[]{:S(2)}) async-start(f32[32,2,16,8,128]{4,3,2,1,0:T(8,128)} %copy-done.8), calls=%async_computation.4 | async-start | bytes 8388608 | tf_op jit(solution)/shard_map/all_to_all | solution.py:364
  318.6 93.1 %copy-start.22 = (bf16[2,512,1024]{2,1,0:T(8,128)(2,1)S(1)}, bf16[2,512,1024]{2,1,0:T(8,128)(2,1)}, u32[]{:S(2)}) copy-start(bf16[2,512,1024]{2,1,0:T(8,128)(2,1)} %constant.36.refs_4_) | copy-start | bytes 6291460
  319.1 63.2 %collective-permute-start.11 = (f32[2,8,128,128]{3,2,1,0:T(8,128)S(1)}, f32[2,8,128,128]{3,2,1,0:T(8,128)S(1)}, u32[]{:S(2)}, u32[]{:S(2)}) collective-permute-start(f32[2,8,128,128]{3,2,1,0:T(8,128)S(1)} %get-tuple-element.43), channel_id=1, source_target_pairs={{0,24},{8,16},{16,8},{24,0},{1,25},{9,17},{17,9},{25,1},{2,26},{10... | collective-permute-start | bytes 3145736 | tf_op jit(solution)/shard_map/ppermute | solution.py:359
  321.7 80.2 %collective-permute-start.10 = (f32[2,8,128,128]{3,2,1,0:T(8,128)S(1)}, f32[2,8,128,128]{3,2,1,0:T(8,128)S(1)}, u32[]{:S(2)}, u32[]{:S(2)}) collective-permute-start(f32[2,8,128,128]{3,2,1,0:T(8,128)S(1)} %get-tuple-element.44), channel_id=1, source_target_pairs={{0,16},{8,24},{16,0},{24,8},{1,17},{9,25},{17,1},{25,9},{2,18},{10... | collective-permute-start | bytes 3145736 | tf_op jit(solution)/shard_map/ppermute | solution.py:359
  322.3 89.4 %collective-permute-start.9 = (f32[2,8,128,128]{3,2,1,0:T(8,128)S(1)}, f32[2,8,128,128]{3,2,1,0:T(8,128)S(1)}, u32[]{:S(2)}, u32[]{:S(2)}) collective-permute-start(f32[2,8,128,128]{3,2,1,0:T(8,128)S(1)} %get-tuple-element.45), channel_id=1, source_target_pairs={{0,8},{8,0},{16,24},{24,16},{1,9},{9,1},{17,25},{25,17},{2,10},{10... | collective-permute-start | bytes 3145736 | tf_op jit(solution)/shard_map/ppermute | solution.py:359
  423.3 2.0 copy-start.11
  425.3 4.0 copy-start
  425.3 4.0 copy-start.1
  425.3 4.1 copy-start.6
  425.3 4.1 copy-start.7
  425.3 99.1 %all-to-all-start.6 = ((f32[32,2,16,8,128]{4,3,2,1,0:T(8,128)}), f32[32,2,16,8,128]{4,3,2,1,0:T(8,128)}, u32[]{:S(2)}, u32[]{:S(2)}) async-start(f32[32,2,16,8,128]{4,3,2,1,0:T(8,128)} %copy-done.11), calls=%async_computation.6 | async-start | bytes 8388608 | tf_op jit(solution)/shard_map/all_to_all | solution.py:364
  441.1 2.0 copy-start.4
  524.4 98.6 %all-to-all-start.1 = ((f32[8,2,16,32,128]{4,3,2,1,0:T(8,128)}), f32[8,2,16,32,128]{4,3,2,1,0:T(8,128)}, u32[]{:S(2)}, u32[]{:S(2)}) async-start(f32[8,2,16,32,128]{4,3,2,1,0:T(8,128)} %copy-done.4), calls=%async_computation.1 | async-start | bytes 8388608 | tf_op jit(solution)/shard_map/all_to_all | solution.py:368
  540.7 2.0 copy-start.5
  623.0 98.8 %all-to-all-start.3 = ((f32[8,2,16,32,128]{4,3,2,1,0:T(8,128)}), f32[8,2,16,32,128]{4,3,2,1,0:T(8,128)}, u32[]{:S(2)}, u32[]{:S(2)}) async-start(f32[8,2,16,32,128]{4,3,2,1,0:T(8,128)} %copy-done.5), calls=%async_computation.3 | async-start | bytes 8388608 | tf_op jit(solution)/shard_map/all_to_all | solution.py:368
  639.4 2.0 copy-start.3
  721.8 98.6 %all-to-all-start.5 = ((f32[8,2,16,32,128]{4,3,2,1,0:T(8,128)}), f32[8,2,16,32,128]{4,3,2,1,0:T(8,128)}, u32[]{:S(2)}, u32[]{:S(2)}) async-start(f32[8,2,16,32,128]{4,3,2,1,0:T(8,128)} %copy-done.3), calls=%async_computation.5 | async-start | bytes 8388608 | tf_op jit(solution)/shard_map/all_to_all | solution.py:368
  738.0 2.0 copy-start.2
  820.3 98.6 %all-to-all-start.7 = ((f32[8,2,16,32,128]{4,3,2,1,0:T(8,128)}), f32[8,2,16,32,128]{4,3,2,1,0:T(8,128)}, u32[]{:S(2)}, u32[]{:S(2)}) async-start(f32[8,2,16,32,128]{4,3,2,1,0:T(8,128)} %copy-done.2), calls=%async_computation.7 | async-start | bytes 8388608 | tf_op jit(solution)/shard_map/all_to_all | solution.py:368
